TPU v7x, 256 devices: a whole 4x4x8 slice. The times are simulated.
256 devices in a mesh: blk: 128 (over y, x, z_lo, core), rep: 2 (over z_hi).
Axes of the slice: x: 4, y: 4, z: 8 (z_hi: 2, z_lo: 4; z = z_hi * 4 + z_lo), core: 2. Of those that a mesh axis runs over, the one named last changes fastest.
Arguments:
- tracks: bfloat16 [131072, 512], P(('blk', 'rep')), may hold values from -80 to 80
Outputs:
- neighbour_sums: bfloat16 [131072, 512], P(('blk', 'rep'))
All inputs are finite; a program needn't handle non-finite values.
Results may differ from a plain program's by a relative error of at most 0.0071.
Values may be sent and summed in bfloat16 or wider, within the bound.
A program may use at most 64 MiB of HBM per device.

v0:
```python
import math

import jax
import jax.numpy as jnp
from jax import lax
from jax.sharding import PartitionSpec as P

STEPS = 3
NS_ITERS = 4
INV_TEMP = 2


EPSILON = 1e-05


def shifted_2(block, axis, distance):
    devices = range(lax.axis_size(axis))
    route = [((i - distance) % len(devices), i) for i in devices]
    return lax.ppermute(block, axis, route)


def combined_all(shard, axis, combine):
    everything = jax.tree.map(lambda part: lax.all_gather(part, axis), shard)
    first = jax.tree.map(lambda part: part[0], everything)

    def hop(k, so_far):
        return combine(so_far, jax.tree.map(lambda part: part[k], everything))

    return lax.fori_loop(1, lax.axis_size(axis), hop, first)


def inverse_root(covariance):
    width = covariance.shape[0]
    identity = jnp.eye(width, dtype=covariance.dtype)
    shifted = covariance + EPSILON * identity
    frobenius = jnp.sqrt(jnp.sum(shifted * shifted))
    iterate = shifted / frobenius
    inverse = identity
    for sweep in range(NS_ITERS):
        factor = 1.5 * identity - 0.5 * jnp.dot(inverse, iterate, precision=lax.Precision.HIGHEST)
        iterate = jnp.dot(iterate, factor, precision=lax.Precision.HIGHEST)
        inverse = jnp.dot(factor, inverse, precision=lax.Precision.HIGHEST)
    return inverse / jnp.sqrt(frobenius)


def attend(state, queries, key_rows, itself, score_scale):
    highest, totals, weighted = state
    scores = (
        lax.dot_general(
            queries, key_rows, (((1,), (1,)), ((), ())), preferred_element_type=jnp.float32
        )
        * score_scale
    )
    scores = jnp.where(itself, -jnp.inf, scores)
    new_high = jnp.maximum(highest, jnp.max(scores, axis=1))
    decay = jnp.exp(highest - new_high)
    expo = jnp.exp(scores - new_high[:, None])
    totals = totals * decay + jnp.sum(expo, axis=1)
    weighted = weighted * decay[:, None] + jnp.dot(
        expo.astype(jnp.bfloat16), key_rows, preferred_element_type=jnp.float32
    )
    return (new_high, totals, weighted)


def combine_parts(first, second):
    high_one, total_one, sum_one = first
    high_two, total_two, sum_two = second
    new_high = jnp.maximum(high_one, high_two)
    scale_one = jnp.exp(high_one - new_high)
    scale_two = jnp.exp(high_two - new_high)
    return (
        new_high,
        total_one * scale_one + total_two * scale_two,
        sum_one * scale_one[..., None] + sum_two * scale_two[..., None],
    )


def empty_state(count, width):
    return (
        jnp.full((count,), -jnp.inf, jnp.float32),
        jnp.zeros((count,), jnp.float32),
        jnp.zeros((count, width), jnp.float32),
    )


def local(tracks):
    local_rows, width = tracks.shape
    n_blk = lax.axis_size("blk")
    n_rep = lax.axis_size("rep")
    track_count = local_rows * n_blk * n_rep
    values = tracks.astype(jnp.float32)
    average = lax.psum(jnp.sum(values, axis=0), ("blk", "rep")) / track_count
    centred = values - average
    covariance = (
        lax.psum(jnp.dot(centred.T, centred, precision=lax.Precision.HIGHEST), ("blk", "rep"))
        / track_count
    )
    whitener = inverse_root(covariance)
    whitened = jnp.dot(centred, whitener, precision=lax.Precision.HIGHEST).astype(jnp.bfloat16)
    group = lax.all_gather(whitened, "rep", axis=0, tiled=True)
    group_size = group.shape[0]
    layer = lax.axis_index("rep")
    score_scale = INV_TEMP / math.sqrt(width)
    key_rows = group
    previous = group
    previous = shifted_2(previous, "blk", 1)
    key_rows = jnp.where(layer == 1, previous, key_rows)
    diagonal = jnp.arange(group_size)[:, None] == jnp.arange(group_size)[None, :]
    state = empty_state(group_size, width)
    for cycle_step in range(STEPS):
        itself = jnp.logical_and(diagonal, jnp.logical_and(layer == 0, cycle_step == 0))
        state = attend(state, group, key_rows, itself, score_scale)
        if cycle_step + 1 < STEPS:
            key_rows = shifted_2(key_rows, "blk", n_rep)
    highest, totals, weighted = combined_all(state, "rep", combine_parts)
    result_rows = weighted / totals[:, None]
    result_rows = lax.dynamic_slice_in_dim(result_rows, layer * local_rows, local_rows, 0)
    return result_rows.astype(jnp.bfloat16)


def solution(mesh):
    in_specs = (P(("blk", "rep"), None),)
    out_specs = P(("blk", "rep"), None)
    return jax.shard_map(local, mesh=mesh, in_specs=in_specs, out_specs=out_specs, check_vma=False)
```

profile of v0, /device:TPU:65, one launch (start us, length us, event | category | flops | bytes accessed | tf_op | source)
XLA Modules:
  0.0 598.2 jit_solution(6219896737983234467)
XLA Ops:
  6.5 1.2 convert_reduce_fusion
  7.7 77.6 %psum.14 = f32[512]{0:T(512)S(1)} all-reduce(f32[512]{0:T(512)S(1)} %convert_reduce_fusion), channel_id=1, replica_groups=mesh['blk'=128,'rep'=2] {'blk','rep'}, use_global_device_ids=true, to_apply=%region_1.0 | all-reduce | flops 512 | bytes 4096 | tf_op jit(solution)/shard_map/psum | solution.py:92
  85.3 4.2 fusion.24
  89.4 0.2 all-gather.6.cloned.1.call-start
  89.7 252.8 %all-reduce.2.cloned.1.call-done = f32[512,512]{1,0:T(8,128)} async-done(((f32[512,512]{1,0:T(8,128)}), f32[512,512]{1,0:T(8,128)}) %all-reduce.2.cloned.1.call-update) | async-done | bytes 1048592 | tf_op jit(solution)/shard_map/psum | solution.py:95
  342.5 2.1 multiply_reduce_fusion.2
  345.4 2.5 select_subtract_fusion.3
  347.8 1.0 fusion.27
  348.8 1.9 fusion.32
  350.7 1.8 select_subtract_fusion.2
  352.6 1.8 fusion.53
  354.5 1.8 fusion.52
  356.3 1.8 select_subtract_fusion.1
  358.2 2.1 fusion.54
  360.3 1.8 fusion.55
  362.1 1.8 select_subtract_fusion
  364.0 1.8 convolution_divide_fusion
  365.9 2.7 convolution_convert_fusion
  368.6 39.0 %all-gather.6.cloned.1.call-done = bf16[1024,512]{1,0:T(8,128)(2,1)} async-done(((bf16[512,512]{1,0:T(8,128)(2,1)}), bf16[1024,512]{1,0:T(8,128)(2,1)}) %all-gather.6.cloned.1.call-update) | async-done | bytes 1048592 | tf_op jit(solution)/shard_map/all_gather | solution.py:100
  407.6 1.4 collective-permute-start
  409.1 12.1 %collective-permute-done = bf16[1024,512]{1,0:T(8,128)(2,1)S(1)} collective-permute-done((bf16[1024,512]{1,0:T(8,128)(2,1)}, bf16[1024,512]{1,0:T(8,128)(2,1)S(1)}, u32[]{:S(2)}, u32[]{:S(2)}) %collective-permute-start) | collective-permute-done | bytes 1048608 | tf_op jit(solution)/shard_map/ppermute | solution.py:19
  421.1 1.3 broadcast_select_fusion
  422.5 3.8 collective-permute-start.1
  426.2 2.5 fusion.7
  428.8 1.3 fusion.12
  430.1 0.6 copy-done
  430.7 17.8 %collective-permute-done.1 = bf16[1024,512]{1,0:T(8,128)(2,1)S(1)} collective-permute-done((bf16[1024,512]{1,0:T(8,128)(2,1)S(1)}, bf16[1024,512]{1,0:T(8,128)(2,1)S(1)}, u32[]{:S(2)}, u32[]{:S(2)}) %collective-permute-start.1) | collective-permute-done | bytes 1048608 | tf_op jit(solution)/shard_map/ppermute | solution.py:19
  448.5 1.9 collective-permute-start.2
  450.4 1.3 multiply_reduce_fusion.1
  451.7 1.3 fusion.10
  453.0 0.6 copy-done.1
  453.6 19.9 %collective-permute-done.2 = bf16[1024,512]{1,0:T(8,128)(2,1)S(1)} collective-permute-done((bf16[1024,512]{1,0:T(8,128)(2,1)S(1)}, bf16[1024,512]{1,0:T(8,128)(2,1)S(1)}, u32[]{:S(2)}, u32[]{:S(2)}) %collective-permute-start.2) | collective-permute-done | bytes 1048608 | tf_op jit(solution)/shard_map/ppermute | solution.py:19
  473.5 1.3 multiply_reduce_fusion
  474.8 2.0 copy-done.3
  476.8 2.8 multiply_add_fusion
  479.6 3.2 fusion.1
  482.8 0.3 copy-done.2
  483.1 0.7 fusion.3
  483.8 0.5 copy-done.4
  484.3 0.7 fusion.5
  485.1 7.1 %all-gather.1 = f32[2,1,1024]{2,1,0:T(1,128)S(1)} all-gather(f32[1,1,1024]{2,1,0:T(1,128)S(1)} %get-tuple-element.38), channel_id=1, replica_groups=mesh['blk'=128,'rep'=2] {'rep'}, dimensions={0}, use_global_device_ids=true | all-gather | bytes 12288 | tf_op jit(solution)/shard_map/all_gather | solution.py:23
  492.2 7.4 %all-gather.2 = f32[2,1,1024]{2,1,0:T(1,128)S(1)} all-gather(f32[1,1,1024]{2,1,0:T(1,128)S(1)} %get-tuple-element.39), channel_id=1, replica_groups=mesh['blk'=128,'rep'=2] {'rep'}, dimensions={0}, use_global_device_ids=true | all-gather | bytes 12288 | tf_op jit(solution)/shard_map/all_gather | solution.py:23
  499.6 0.1 dynamic-slice.2
  499.7 0.1 dynamic-slice
  499.8 0.1 dynamic-slice.1
  499.9 88.1 %all-gather.8.cloned.1.call-done = f32[2048,512]{1,0:T(8,128)} async-done(((f32[1024,512]{1,0:T(8,128)}), f32[2048,512]{1,0:T(8,128)}) %all-gather.8.cloned.1.call-update) | async-done | bytes 4194320 | tf_op jit(solution)/shard_map/all_gather | solution.py:23
  587.9 2.7 fusion.49
  590.6 1.1 fusion.28
  (23 shorter events, 0.2 us)
Async XLA Ops:
  6.5 336.0 %all-reduce.2.cloned.1.call-start = ((), (), s32[]{:S(2)}) async-start(), calls=%async_computation | async-start | bytes 2097152 | tf_op jit(solution)/shard_map/psum | solution.py:95
  89.4 318.2 %all-gather.6.cloned.1.call-start = ((), (), s32[]{:S(2)}) async-start(), calls=%async_computation.1 | async-start | bytes 1572864 | tf_op jit(solution)/shard_map/all_gather | solution.py:100
  345.3 3.5 copy-start.7
  362.1 3.7 copy-start.5
  368.6 219.4 %all-gather.8.cloned.1.call-start = ((), (), s32[]{:S(2)}) async-start(), calls=%async_computation.2 | async-start | bytes 6291456 | tf_op jit(solution)/shard_map/all_gather | solution.py:23
  407.6 13.5 %collective-permute-start = (bf16[1024,512]{1,0:T(8,128)(2,1)}, bf16[1024,512]{1,0:T(8,128)(2,1)S(1)}, u32[]{:S(2)}, u32[]{:S(2)}) collective-permute-start(bf16[1024,512]{1,0:T(8,128)(2,1)} %all-gather.6.cloned.1.call-done), channel_id=1, source_target_pairs={{254,0},{0,2},{2,4},{4,6},{6,8},{8,10},{10,12},{12,14},{14,16},{16... | collective-permute-start | bytes 3145736 | tf_op jit(solution)/shard_map/ppermute | solution.py:19
  422.5 26.0 %collective-permute-start.1 = (bf16[1024,512]{1,0:T(8,128)(2,1)S(1)}, bf16[1024,512]{1,0:T(8,128)(2,1)S(1)}, u32[]{:S(2)}, u32[]{:S(2)}) collective-permute-start(bf16[1024,512]{1,0:T(8,128)(2,1)S(1)} %broadcast_select_fusion), channel_id=1, source_target_pairs={{252,0},{254,2},{0,4},{2,6},{4,8},{6,10},{8,12},{10,14},{12,16},{1... | collective-permute-start | bytes 3145736 | tf_op jit(solution)/shard_map/ppermute | solution.py:19
  428.7 1.9 copy-start
  428.7 21.6 %copy-start.6 = (bf16[1024,512]{1,0:T(8,128)(2,1)S(1)}, bf16[1024,512]{1,0:T(8,128)(2,1)}, u32[]{:S(2)}) copy-start(bf16[1024,512]{1,0:T(8,128)(2,1)} %all-gather.6.cloned.1.call-done) | copy-start | bytes 3145732
  448.5 25.0 %collective-permute-start.2 = (bf16[1024,512]{1,0:T(8,128)(2,1)S(1)}, bf16[1024,512]{1,0:T(8,128)(2,1)S(1)}, u32[]{:S(2)}, u32[]{:S(2)}) collective-permute-start(bf16[1024,512]{1,0:T(8,128)(2,1)S(1)} %collective-permute-done.1), channel_id=1, source_target_pairs={{252,0},{254,2},{0,4},{2,6},{4,8},{6,10},{8,12},{10,14},{12,16},{1... | collective-permute-start | bytes 3145736 | tf_op jit(solution)/shard_map/ppermute | solution.py:19
  451.7 2.0 copy-start.1
  474.8 2.0 copy-start.3
  479.6 3.5 copy-start.2
  479.6 4.7 copy-start.4
Sparse Core Ops, SparseCore 0:
  89.6 252.8 all-reduce.1
  368.7 38.8 all-gather.5
  479.7 108.1 all-gather.7
where the time goes:
time: 603 us; the launch traced here: 598 us
  waiting for transfers between devices  430 us (71%)
  blocking collectives  92.1 us (15%)
  matrix products  37.7 us (6%)
  between operations  14.1 us (2%)
  other arithmetic  10.4 us (2%)
  starting transfers between devices  7.39 us (1%)
  local copies, waits for them, and re-layouts  6.91 us (1%)
    psum x1, waiting for transfers between devices, local(): lax.psum(jnp.dot(centred.T, centred, precision=lax.Precision.HIGHEST), ('...  253 us
    all_gather x1, waiting for transfers between devices, combined_all(): everything = jax.tree.map(lambda part: lax.all_gather(part, axis), shard)  88.1 us
    psum x1, blocking collectives, local(): average = lax.psum(jnp.sum(values, axis=0), ('blk', 'rep')) / track_count  77.6 us
    ppermute x3, waiting for transfers between devices, shifted_2(): return lax.ppermute(block, axis, route)  49.7 us
    all_gather x1, waiting for transfers between devices, local(): group = lax.all_gather(whitened, 'rep', axis=0, tiled=True)  39 us
    all_gather x2, blocking collectives, combined_all(): everything = jax.tree.map(lambda part: lax.all_gather(part, axis), shard)  14.5 us
  transfers between devices with their start and end apart: 6, of which 6 were waited for; matrix products, arithmetic and copies ran while one was open for 2% of the time, Pallas kernels for 0%

commit v1 on v0

v1 whole, which is shorter than its diff:
```python
import functools
import math

import jax
import jax.numpy as jnp
from jax import lax
from jax.experimental import pallas as pl
from jax.experimental.pallas import tpu as pltpu
from jax.sharding import PartitionSpec as P

NS_ITERS = 4
INV_TEMP = 2
EPSILON = 1e-05
WIDTH = 512
ROWS = 512
TRACKS = 131072
MESH = pl.DeviceIdType.MESH
F32 = jnp.float32
BF16 = jnp.bfloat16

TILES = [(i, j) for i in range(4) for j in range(i, 4)]
HALF = 640
PART = 40
PLANE = [(dy, dx) for dy in range(4) for dx in range(4)][1:]

OWN, BACK, RING, SIDE, MATE, MATE_RING = 0, 0, 4, 8, 12, 15
SLOTS = 18
CHUNKS = 2
CHUNK = ROWS // CHUNKS


def place(y, x, z, core):
    return (((y * 4 + x) * 4 + z % 4) * 2 + core, z // 4)


def split(value):
    high = value.astype(BF16)
    return high, (value - high.astype(F32)).astype(BF16)


def dot(left, right):
    return jnp.dot(left, right, preferred_element_type=F32)


def product(left, right):
    return dot(left[0], right[0]) + (dot(left[0], right[1]) + dot(left[1], right[0]))


def kernel(
    tracks_ref, out_ref, keys, halves, from_mate, outgoing, plane_in, line_out, line_in, full,
    iterate, inverse, scores, weighted, queries, whitener, load_sem, ring_send, ring_recv,
    back_send, back_recv, side_send, side_recv, mate_send, mate_recv, core_send, core_recv,
    plane_send, plane_recv, line_send, line_recv, gather_send, gather_recv, whole_send, whole_recv,
):
    group = lax.axis_index("blk")
    rep = lax.axis_index("rep")
    y, x, core = group // 32, (group // 8) % 4, group % 2
    step_z = (group // 2) % 4
    z = rep * 4 + step_z
    mine = y * 4 + x
    wrap = (x + 1) // 4
    next_y, next_x = (y + wrap) % 4, (x + 1) % 4
    back_wrap = (4 - x) // 4
    last_y, last_x = (y + 3 * back_wrap) % 4, (x + 3) % 4
    mate = place(y, x, z, 1 - core)
    down = place(y, x, (z + 7) % 8, core)
    column = place(next_y, next_x, z, core)
    at_end = (step_z + 1) // 4
    at_start = (4 - step_z) // 4
    ahead = place(
        at_end * next_y + (1 - at_end) * y, at_end * next_x + (1 - at_end) * x, (z + 1) % 8, core
    )
    behind = place(
        at_start * last_y + (1 - at_start) * y,
        at_start * last_x + (1 - at_start) * x,
        (z + 7) % 8,
        core,
    )

    load = pltpu.make_async_copy(tracks_ref, keys.at[OWN], load_sem)
    load.start()
    barrier = pltpu.get_barrier_semaphore()

    def greet(device):
        pl.semaphore_signal(barrier, inc=1, device_id=device, device_id_type=MESH)

    greet(mate)
    for dz in range(1, 8):
        greet(place(y, x, (z + dz) % 8, core))
    for dy, dx in PLANE:
        greet(place((y + dy) % 4, (x + dx) % 4, z, core))

    @pl.when(at_end == 1)
    def _():
        greet(ahead)

    @pl.when(at_start == 1)
    def _():
        greet(behind)

    load.wait()

    rows = keys[OWN]
    gram = lax.dot_general(rows, rows, (((0,), (0,)), ((), ())), preferred_element_type=F32)
    for n, (i, j) in enumerate(TILES):
        halves[n // 5, pl.ds(128 * (n % 5), 128), :] = gram[
            128 * i : 128 * (i + 1), 128 * j : 128 * (j + 1)
        ]
    sums = jnp.sum(rows.astype(F32), axis=0, keepdims=True)
    tail = jnp.concatenate(
        [sums[:, 128 * i : 128 * (i + 1)] for i in range(4)] + [jnp.zeros((4, 128), F32)], axis=0
    )
    for h in range(2):
        halves[h, pl.ds(HALF, 8), :] = tail

    pl.semaphore_wait(barrier, 23 + at_end + at_start)

    def piece(slot, part):
        return keys.at[slot, pl.ds(part * CHUNK, CHUNK)]

    def mover(source, target, part, send, recv, device):
        return pltpu.make_async_remote_copy(
            src_ref=piece(source, part),
            dst_ref=piece(target, part),
            send_sem=send,
            recv_sem=recv,
            device_id=device,
            device_id_type=MESH,
        )

    def ring_hop(s, part):
        source = OWN if s == 3 else RING + s + 1
        return mover(
            source, RING + s, part, ring_send.at[s, part], ring_recv.at[s, part], down
        )

    def back_hop(s, part):
        return mover(
            BACK + s - 1, BACK + s, part, back_send.at[s, part], back_recv.at[s, part], ahead
        )

    def side_hop(s, part):
        return mover(
            RING + s, SIDE + s, part, side_send.at[s, part], side_recv.at[s, part], column
        )

    def used(s):
        return RING + s + 4 * jnp.minimum(jnp.maximum(s - step_z, 0), 1)

    def mate_back(i, part):
        return mover(
            BACK + core + i, MATE + i, part, mate_send.at[i, part], mate_recv.at[i, part], mate
        )

    def mate_ring(i, part):
        return mover(
            used(core + i), MATE_RING + i, part,
            mate_send.at[3 + i, part], mate_recv.at[3 + i, part], mate,
        )

    def each(act):
        for part in range(CHUNKS):
            act(part)

    def sides(s, act):
        cond = step_z < s
        if s == 3:
            cond = jnp.logical_and(cond, core == 1)

        @pl.when(cond)
        def _():
            act()

    def start_own():
        each(lambda part: ring_hop(3, part).start())
        each(lambda part: back_hop(1, part).start())

    def pass_ring(s, part):
        ring_hop(s, part).wait_recv()
        if s > 0:
            ring_hop(s - 1, part).start()
            sides(s, lambda: side_hop(s, part).start())

    def pass_back(s, part):
        back_hop(s, part).wait_recv()
        if s == 1:
            back_hop(2, part).start()
        if s == 2:

            @pl.when(core == 1)
            def _():
                back_hop(3, part).start()

    start_core = pltpu.make_async_remote_copy(
        src_ref=halves.at[1 - core], dst_ref=from_mate, send_sem=core_send, recv_sem=core_recv,
        device_id=mate, device_id_type=MESH,
    )
    start_core.start()
    start_own()
    start_core.wait_recv()
    chip = halves[core] + from_mate[...]
    for q in range(16):
        outgoing[q, pl.ds(0, PART), :] = chip[PART * q : PART * (q + 1)]
        outgoing[q, pl.ds(PART, 8), :] = chip[HALF : HALF + 8]

    def plane_hop(n, dy, dx):
        ty, tx = (y + dy) % 4, (x + dx) % 4
        return pltpu.make_async_remote_copy(
            src_ref=outgoing.at[ty * 4 + tx], dst_ref=plane_in.at[n], send_sem=plane_send,
            recv_sem=plane_recv, device_id=place(ty, tx, z, core), device_id_type=MESH,
        )

    for n, (dy, dx) in enumerate(PLANE):
        plane_hop(n, dy, dx).start()
    pltpu.make_async_copy(plane_in, plane_in, plane_recv).wait()
    line_out[...] = outgoing[mine] + jnp.sum(plane_in[...], axis=0)

    def line_hop(dz):
        return pltpu.make_async_remote_copy(
            src_ref=line_out, dst_ref=line_in.at[dz - 1], send_sem=line_send, recv_sem=line_recv,
            device_id=place(y, x, (z + dz) % 8, core), device_id_type=MESH,
        )

    for dz in range(1, 8):
        line_hop(dz).start()
    each(lambda part: pass_ring(3, part))
    each(lambda part: pass_back(1, part))
    pltpu.make_async_copy(line_in, line_in, line_recv).wait()
    total = line_out[...] + jnp.sum(line_in[...], axis=0)
    full[core, pl.ds(pl.multiple_of(PART * mine, 8), PART), :] = total[:PART]
    average = total[PART : PART + 4] / TRACKS

    def gather_hop(dy, dx):
        area = full.at[core, pl.ds(pl.multiple_of(PART * mine, 8), PART)]
        return pltpu.make_async_remote_copy(
            src_ref=area, dst_ref=area, send_sem=gather_send, recv_sem=gather_recv,
            device_id=place((y + dy) % 4, (x + dx) % 4, z, core), device_id_type=MESH,
        )

    for dy, dx in PLANE:
        gather_hop(dy, dx).start()
    each(lambda part: pass_ring(2, part))
    each(lambda part: pass_back(2, part))
    others = full.at[core, pl.ds(0, PART * 15)]
    pltpu.make_async_copy(others, others, gather_recv).wait()
    whole = pltpu.make_async_remote_copy(
        src_ref=full.at[core], dst_ref=full.at[core], send_sem=whole_send, recv_sem=whole_recv,
        device_id=mate, device_id_type=MESH,
    )
    whole.start()
    whole.wait()

    square = jnp.zeros((1, 1), F32)
    row_id = lax.broadcasted_iota(jnp.int32, (128, 128), 0)
    col_id = lax.broadcasted_iota(jnp.int32, (128, 128), 1)
    eye = (row_id == col_id).astype(F32)
    upright = [jnp.broadcast_to(average[i : i + 1], (128, 128)).T for i in range(4)]
    for n, (i, j) in enumerate(TILES):
        tile = full[n // 5, pl.ds(128 * (n % 5), 128), :] / TRACKS - upright[i] * average[j : j + 1]
        if i == j:
            tile = tile + EPSILON * eye
        part = jnp.sum(jnp.sum(tile * tile, axis=0, keepdims=True), axis=1, keepdims=True)
        square = square + (part if i == j else 2.0 * part)
        iterate[pl.ds(128 * i, 128), pl.ds(128 * j, 128)] = tile
        if i != j:
            iterate[pl.ds(128 * j, 128), pl.ds(128 * i, 128)] = tile.T
    frobenius = jnp.sqrt(square)
    iterate[...] = iterate[...] / frobenius

    full_row = lax.broadcasted_iota(jnp.int32, (WIDTH, WIDTH), 0)
    full_col = lax.broadcasted_iota(jnp.int32, (WIDTH, WIDTH), 1)
    diagonal = full_row == full_col

    def factor_of(matrix):
        return jnp.where(diagonal, 1.5, 0.0) - 0.5 * matrix

    for sweep in range(NS_ITERS - 1):
        factor = split(factor_of(iterate[...]))
        if sweep == 0:
            inverse[...] = factor_of(iterate[...])
        else:
            inverse[...] = product(split(inverse[...]), factor)
        iterate[...] = product(split(iterate[...]), split(product(factor, factor)))
        if sweep == 0:
            each(lambda part: pass_ring(1, part))
    unscaled = product(split(inverse[...]), split(factor_of(iterate[...])))
    whitener[...] = unscaled / jnp.sqrt(frobenius)
    weights = split(whitener[...])
    centre = jnp.concatenate([average[i : i + 1] for i in range(4)], axis=1)
    centred = keys[OWN].astype(F32) - centre
    turned = product(split(product(split(centred), weights)), weights)
    queries[...] = (turned * (INV_TEMP / math.sqrt(WIDTH) * math.log2(math.e))).astype(BF16)

    @pl.when(core == 1)
    def _():
        each(lambda part: back_hop(3, part).wait_recv())

    for i in range(3):
        each(lambda part: mate_back(i, part).start())
    for s in range(1, 4):
        sides(s, lambda: each(lambda part: side_hop(s, part).wait_recv()))
    each(lambda part: pass_ring(0, part))
    for i in range(3):
        each(lambda part: mate_ring(i, part).start())
    for i in range(3):
        each(lambda part: mate_back(i, part).wait_recv())
        each(lambda part: mate_ring(i, part).wait_recv())

    def key_slot(n):
        return jnp.where(n < 3, n, jnp.where(n < 6, used(n - 3), n + 6))

    def score(n, high):
        found = lax.dot_general(
            queries[...], keys[key_slot(n)], (((1,), (1,)), ((), ())), preferred_element_type=F32
        )
        found = jnp.where(jnp.logical_and(diagonal, n == 0), -jnp.inf, found)
        scores[n] = found
        for i in range(4):
            high = jnp.maximum(high, found[:, 128 * i : 128 * (i + 1)])
        return high

    high = lax.fori_loop(0, 12, score, jnp.full((ROWS, 128), -jnp.inf, F32))
    highest = jnp.max(high, axis=1, keepdims=True)
    weighted[...] = jnp.zeros_like(weighted)

    def spread(n, totals):
        weight = jnp.exp2(scores[n] - highest).astype(BF16)
        weighted[...] += dot(weight, keys[key_slot(n)])
        wide = weight.astype(F32)
        for i in range(4):
            totals = totals + wide[:, 128 * i : 128 * (i + 1)]
        return totals

    totals = lax.fori_loop(0, 12, spread, jnp.zeros((ROWS, 128), F32))
    totals = jnp.sum(totals, axis=1, keepdims=True)
    mixed = weighted[...] / totals - centre
    out_ref[...] = product(split(mixed), split(whitener[...])).astype(BF16)

    start_core.wait_send()
    pltpu.make_async_copy(plane_in, plane_in, plane_send).wait()
    pltpu.make_async_copy(line_in, line_in, line_send).wait()
    pltpu.make_async_copy(others, others, gather_send).wait()
    for part in range(CHUNKS):
        for s in range(4):
            ring_hop(s, part).wait_send()
        back_hop(1, part).wait_send()
        back_hop(2, part).wait_send()
        for i in range(3):
            mate_back(i, part).wait_send()
            mate_ring(i, part).wait_send()
    for s in range(1, 4):
        sides(s, lambda: each(lambda part: side_hop(s, part).wait_send()))

    @pl.when(core == 1)
    def _():
        each(lambda part: back_hop(3, part).wait_send())


def local(tracks):
    dma = pltpu.SemaphoreType.DMA
    return pl.pallas_call(
        kernel,
        out_shape=jax.ShapeDtypeStruct((ROWS, WIDTH), BF16),
        in_specs=[pl.BlockSpec(memory_space=pl.ANY)],
        out_specs=pl.BlockSpec(memory_space=pltpu.VMEM),
        scratch_shapes=[
            pltpu.VMEM((SLOTS, ROWS, WIDTH), BF16),
            pltpu.VMEM((2, HALF + 8, 128), F32),
            pltpu.VMEM((HALF + 8, 128), F32),
            pltpu.VMEM((16, PART + 8, 128), F32),
            pltpu.VMEM((15, PART + 8, 128), F32),
            pltpu.VMEM((PART + 8, 128), F32),
            pltpu.VMEM((7, PART + 8, 128), F32),
            pltpu.VMEM((2, HALF, 128), F32),
            pltpu.VMEM((WIDTH, WIDTH), F32),
            pltpu.VMEM((WIDTH, WIDTH), F32),
            pltpu.VMEM((12, ROWS, ROWS), F32),
            pltpu.VMEM((ROWS, WIDTH), F32),
            pltpu.VMEM((ROWS, WIDTH), BF16),
            pltpu.VMEM((WIDTH, WIDTH), F32),
            dma(()),
            dma((4, CHUNKS)), dma((4, CHUNKS)),
            dma((4, CHUNKS)), dma((4, CHUNKS)),
            dma((4, CHUNKS)), dma((4, CHUNKS)),
            dma((6, CHUNKS)), dma((6, CHUNKS)),
            dma(()), dma(()), dma(()), dma(()), dma(()), dma(()), dma(()), dma(()), dma(()), dma(()),
        ],
        compiler_params=pltpu.CompilerParams(
            collective_id=0, has_side_effects=True, vmem_limit_bytes=56 * 1024 * 1024
        ),
    )(tracks)


def solution(mesh):
    spec = P(("blk", "rep"), None)
    return jax.shard_map(local, mesh=mesh, in_specs=(spec,), out_specs=spec, check_vma=False)
```

time: 603 us -> 98.9 us (0.16)
  the two profiles are of different devices: /device:TPU:65 before, /device:TPU:3 now
where the time goes in v1:
time: 98.9 us; the launch traced here: 98.7 us
  Pallas kernels  96.8 us (98%)
  local copies, waits for them, and re-layouts  1.87 us (2%)
    pallas_call x1, Pallas kernels, local(): pl.pallas_call(kernel, out_shape=jax.ShapeDtypeStruct((ROWS, WIDTH), BF16...  96.8 us

profile of v1, /device:TPU:3, one launch (start us, length us, event | category | flops | bytes accessed | tf_op | source)
XLA Modules:
  0.0 98.7 jit_solution(12610342085366371290)
XLA Ops:
  0.0 96.8 %shard_map.17 = bf16[512,512]{1,0:T(8,128)(2,1)} custom-call(bf16[512,512]{1,0:T(8,128)(2,1)} %tracks_ref.1), custom_call_target="tpu_custom_call" | custom-call | tf_op jit(solution)/shard_map/pallas_call | solution.py:361
  96.8 1.9 %copy.3 = bf16[512,512]{1,0:T(8,128)(2,1)} copy(bf16[512,512]{1,0:T(8,128)(2,1)} %shard_map.17) | data formatting | bytes 1048576

commit v2 on v1

--- a/solution.py
+++ b/solution.py
@@ -60,22 +60,11 @@
     mine = y * 4 + x
     wrap = (x + 1) // 4
     next_y, next_x = (y + wrap) % 4, (x + 1) % 4
-    back_wrap = (4 - x) // 4
-    last_y, last_x = (y + 3 * back_wrap) % 4, (x + 3) % 4
     mate = place(y, x, z, 1 - core)
     down = place(y, x, (z + 7) % 8, core)
     column = place(next_y, next_x, z, core)
+    up = place(y, x, (z + 1) % 8, core)
     at_end = (step_z + 1) // 4
-    at_start = (4 - step_z) // 4
-    ahead = place(
-        at_end * next_y + (1 - at_end) * y, at_end * next_x + (1 - at_end) * x, (z + 1) % 8, core
-    )
-    behind = place(
-        at_start * last_y + (1 - at_start) * y,
-        at_start * last_x + (1 - at_start) * x,
-        (z + 7) % 8,
-        core,
-    )
 
     load = pltpu.make_async_copy(tracks_ref, keys.at[OWN], load_sem)
     load.start()
@@ -89,14 +78,6 @@
         greet(place(y, x, (z + dz) % 8, core))
     for dy, dx in PLANE:
         greet(place((y + dy) % 4, (x + dx) % 4, z, core))
-
-    @pl.when(at_end == 1)
-    def _():
-        greet(ahead)
-
-    @pl.when(at_start == 1)
-    def _():
-        greet(behind)
 
     load.wait()
 
@@ -113,7 +94,7 @@
     for h in range(2):
         halves[h, pl.ds(HALF, 8), :] = tail
 
-    pl.semaphore_wait(barrier, 23 + at_end + at_start)
+    pl.semaphore_wait(barrier, 23)
 
     def piece(slot, part):
         return keys.at[slot, pl.ds(part * CHUNK, CHUNK)]
@@ -135,13 +116,15 @@
         )
 
     def back_hop(s, part):
+        source = BACK + s - 1 + at_end * (SIDE - BACK + 1)
         return mover(
-            BACK + s - 1, BACK + s, part, back_send.at[s, part], back_recv.at[s, part], ahead
+            source, BACK + s, part, back_send.at[s, part], back_recv.at[s, part], up
         )
 
     def side_hop(s, part):
+        source = RING + s + at_end * (BACK - 1 - RING)
         return mover(
-            RING + s, SIDE + s, part, side_send.at[s, part], side_recv.at[s, part], column
+            source, SIDE + s, part, side_send.at[s, part], side_recv.at[s, part], column
         )
 
     def used(s):
@@ -162,41 +145,71 @@
         for part in range(CHUNKS):
             act(part)
 
-    def sides(s, act):
-        cond = step_z < s
-        if s == 3:
-            cond = jnp.logical_and(cond, core == 1)
-
+    def start_mate_back(i):
+        each(lambda part: mate_back(i, part).start())
+
+    def start_mate_ring(i):
+        each(lambda part: mate_ring(i, part).start())
+
+    def when(cond, act):
         @pl.when(cond)
         def _():
             act()
 
-    def start_own():
-        each(lambda part: ring_hop(3, part).start())
-        each(lambda part: back_hop(1, part).start())
+    inner = step_z < 3
+    last = step_z == 3
+    second = core == 1
+
+    both = jnp.logical_and
+
+    def lower(s):
+        return both(step_z < s, second) if s == 3 else step_z < s
+
+    def start_own(part):
+        ring_hop(3, part).start()
+        when(inner, lambda: back_hop(1, part).start())
+
+    def take_ring(s, part):
+        ring_hop(s, part).wait_recv()
+
+    def send_ring(s, part):
+        ring_hop(s - 1, part).start()
 
     def pass_ring(s, part):
-        ring_hop(s, part).wait_recv()
-        if s > 0:
-            ring_hop(s - 1, part).start()
-            sides(s, lambda: side_hop(s, part).start())
-
-    def pass_back(s, part):
-        back_hop(s, part).wait_recv()
-        if s == 1:
-            back_hop(2, part).start()
-        if s == 2:
-
-            @pl.when(core == 1)
-            def _():
-                back_hop(3, part).start()
+        take_ring(s, part)
+        send_ring(s, part)
+
+    def drop(s, part):
+        when(lower(s), lambda: side_hop(s, part).start())
+
+    def lift(s, part):
+        when(both(last, second) if s == 3 else last, lambda: side_hop(s, part).start())
+
+    def pass_end(s, part):
+        def go():
+            side_hop(s, part).wait_recv()
+            back_hop(s, part).start()
+
+        when(both(last, second) if s == 3 else last, go)
+
+    def pass_back(s, part, here):
+        def go():
+            back_hop(s, part).wait_recv()
+            if s < 3:
+                sends = both(inner, second) if s == 2 else inner
+                when(sends, lambda: back_hop(s + 1, part).start())
+
+        when(both(here, second) if s == 3 else here, go)
+
+    def take_side(s, part):
+        when(lower(s), lambda: side_hop(s, part).wait_recv())
 
     start_core = pltpu.make_async_remote_copy(
         src_ref=halves.at[1 - core], dst_ref=from_mate, send_sem=core_send, recv_sem=core_recv,
         device_id=mate, device_id_type=MESH,
     )
     start_core.start()
-    start_own()
+    each(start_own)
     start_core.wait_recv()
     chip = halves[core] + from_mate[...]
     for q in range(16):
@@ -212,6 +225,7 @@
 
     for n, (dy, dx) in enumerate(PLANE):
         plane_hop(n, dy, dx).start()
+    each(lambda part: lift(1, part))
     pltpu.make_async_copy(plane_in, plane_in, plane_recv).wait()
     line_out[...] = outgoing[mine] + jnp.sum(plane_in[...], axis=0)
 
@@ -223,8 +237,11 @@
 
     for dz in range(1, 8):
         line_hop(dz).start()
-    each(lambda part: pass_ring(3, part))
-    each(lambda part: pass_back(1, part))
+    for part in range(CHUNKS):
+        pass_back(1, part, last)
+        lift(2, part)
+        take_ring(3, part)
+        drop(3, part)
     pltpu.make_async_copy(line_in, line_in, line_recv).wait()
     total = line_out[...] + jnp.sum(line_in[...], axis=0)
     full[core, pl.ds(pl.multiple_of(PART * mine, 8), PART), :] = total[:PART]
@@ -239,8 +256,11 @@
 
     for dy, dx in PLANE:
         gather_hop(dy, dx).start()
-    each(lambda part: pass_ring(2, part))
-    each(lambda part: pass_back(2, part))
+    for part in range(CHUNKS):
+        send_ring(3, part)
+        pass_end(1, part)
+        pass_back(1, part, both(step_z > 0, inner))
+    each(lambda part: pass_end(2, part))
     others = full.at[core, pl.ds(0, PART * 15)]
     pltpu.make_async_copy(others, others, gather_recv).wait()
     whole = pltpu.make_async_remote_copy(
@@ -248,6 +268,13 @@
         device_id=mate, device_id_type=MESH,
     )
     whole.start()
+    for part in range(CHUNKS):
+        pass_ring(2, part)
+        pass_back(1, part, step_z == 0)
+        pass_back(2, part, step_z > 1)
+        lift(3, part)
+        drop(2, part)
+    start_mate_back(0)
     whole.wait()
 
     square = jnp.zeros((1, 1), F32)
@@ -281,57 +308,85 @@
         else:
             inverse[...] = product(split(inverse[...]), factor)
         iterate[...] = product(split(iterate[...]), split(product(factor, factor)))
-        if sweep == 0:
-            each(lambda part: pass_ring(1, part))
+        if sweep == 1:
+            pass_ring(1, 0)
+            drop(1, 0)
+        if sweep == 2:
+            pass_end(3, 0)
     unscaled = product(split(inverse[...]), split(factor_of(iterate[...])))
     whitener[...] = unscaled / jnp.sqrt(frobenius)
+    pass_ring(1, 1)
+    drop(1, 1)
     weights = split(whitener[...])
     centre = jnp.concatenate([average[i : i + 1] for i in range(4)], axis=1)
     centred = keys[OWN].astype(F32) - centre
     turned = product(split(product(split(centred), weights)), weights)
     queries[...] = (turned * (INV_TEMP / math.sqrt(WIDTH) * math.log2(math.e))).astype(BF16)
 
-    @pl.when(core == 1)
-    def _():
-        each(lambda part: back_hop(3, part).wait_recv())
-
-    for i in range(3):
-        each(lambda part: mate_back(i, part).start())
-    for s in range(1, 4):
-        sides(s, lambda: each(lambda part: side_hop(s, part).wait_recv()))
-    each(lambda part: pass_ring(0, part))
-    for i in range(3):
-        each(lambda part: mate_ring(i, part).start())
-    for i in range(3):
-        each(lambda part: mate_back(i, part).wait_recv())
-        each(lambda part: mate_ring(i, part).wait_recv())
+    order = [
+        BACK, BACK + 1, MATE, used(2), MATE_RING + 2, BACK + 2, MATE + 1,
+        used(1), RING, MATE_RING + 1, MATE_RING, MATE + 2,
+    ]
 
     def key_slot(n):
-        return jnp.where(n < 3, n, jnp.where(n < 6, used(n - 3), n + 6))
+        return sum(jnp.where(n == i, slot, 0) for i, slot in enumerate(order))
 
     def score(n, high):
         found = lax.dot_general(
             queries[...], keys[key_slot(n)], (((1,), (1,)), ((), ())), preferred_element_type=F32
         )
-        found = jnp.where(jnp.logical_and(diagonal, n == 0), -jnp.inf, found)
+        found = jnp.where(both(diagonal, n == 0), -jnp.inf, found)
         scores[n] = found
         for i in range(4):
             high = jnp.maximum(high, found[:, 128 * i : 128 * (i + 1)])
         return high
 
-    high = lax.fori_loop(0, 12, score, jnp.full((ROWS, 128), -jnp.inf, F32))
-    highest = jnp.max(high, axis=1, keepdims=True)
+    def attend(state, start, stop):
+        before, totals = state
+        high = jnp.broadcast_to(before, (ROWS, 128))
+        high = lax.fori_loop(start, stop, score, high)
+        highest = jnp.max(high, axis=1, keepdims=True)
+        if start > 0:
+            decay = jnp.exp2(before - highest)
+            weighted[...] = weighted[...] * decay
+            totals = totals * decay
+
+        def spread(n, totals):
+            weight = jnp.exp2(scores[n] - highest).astype(BF16)
+            weighted[...] += dot(weight, keys[key_slot(n)])
+            wide = weight.astype(F32)
+            for i in range(4):
+                totals = totals + wide[:, 128 * i : 128 * (i + 1)]
+            return totals
+
+        return highest, lax.fori_loop(start, stop, spread, totals)
+
+    pass_end(3, 1)
+    for part in range(CHUNKS):
+        pass_back(2, part, step_z < 2)
+        take_side(3, part)
+        take_side(2, part)
+    start_mate_back(1)
+    start_mate_ring(2)
+    each(lambda part: mate_back(0, part).wait_recv())
     weighted[...] = jnp.zeros_like(weighted)
-
-    def spread(n, totals):
-        weight = jnp.exp2(scores[n] - highest).astype(BF16)
-        weighted[...] += dot(weight, keys[key_slot(n)])
-        wide = weight.astype(F32)
-        for i in range(4):
-            totals = totals + wide[:, 128 * i : 128 * (i + 1)]
-        return totals
-
-    totals = lax.fori_loop(0, 12, spread, jnp.zeros((ROWS, 128), F32))
+    state = (jnp.full((ROWS, 1), -jnp.inf, F32), jnp.zeros((ROWS, 128), F32))
+    state = attend(state, 0, 3)
+    each(lambda part: mate_back(1, part).wait_recv())
+    each(lambda part: mate_ring(2, part).wait_recv())
+    state = attend(state, 3, 7)
+    each(lambda part: take_side(1, part))
+    start_mate_ring(1)
+    when(second, lambda: start_mate_ring(0))
+    each(lambda part: take_ring(0, part))
+    when(core == 0, lambda: start_mate_ring(0))
+    each(lambda part: pass_back(3, part, step_z >= 0))
+    start_mate_back(2)
+    state = attend(state, 7, 9)
+    each(lambda part: mate_ring(1, part).wait_recv())
+    each(lambda part: mate_ring(0, part).wait_recv())
+    each(lambda part: mate_back(2, part).wait_recv())
+    _, totals = attend(state, 9, 12)
     totals = jnp.sum(totals, axis=1, keepdims=True)
     mixed = weighted[...] / totals - centre
     out_ref[...] = product(split(mixed), split(whitener[...])).astype(BF16)
@@ -343,17 +398,15 @@
     for part in range(CHUNKS):
         for s in range(4):
             ring_hop(s, part).wait_send()
-        back_hop(1, part).wait_send()
-        back_hop(2, part).wait_send()
         for i in range(3):
             mate_back(i, part).wait_send()
             mate_ring(i, part).wait_send()
-    for s in range(1, 4):
-        sides(s, lambda: each(lambda part: side_hop(s, part).wait_send()))
-
-    @pl.when(core == 1)
-    def _():
-        each(lambda part: back_hop(3, part).wait_send())
+        for s in range(1, 4):
+            gone = jnp.logical_or(lower(s), both(last, second) if s == 3 else last)
+            when(gone, lambda: side_hop(s, part).wait_send())
+        back_hop(1, part).wait_send()
+        back_hop(2, part).wait_send()
+        when(second, lambda: back_hop(3, part).wait_send())
 
 
 def local(tracks):

time: 98.9 us -> 78.7 us (0.80)
  the two profiles are of different devices: /device:TPU:3 before, /device:TPU:65 now
where the time goes in v2:
time: 78.7 us; the launch traced here: 78.6 us
  Pallas kernels  76.7 us (97%)
  local copies, waits for them, and re-layouts  1.87 us (2%)
    pallas_call x1, Pallas kernels, local(): pl.pallas_call(kernel, out_shape=jax.ShapeDtypeStruct((ROWS, WIDTH), BF16...  76.7 us
    unnamed x1, local copies, waits for them, and re-layouts  1.87 us

profile of v2, /device:TPU:65, one launch (start us, length us, event | category | flops | bytes accessed | tf_op | source)
XLA Modules:
  0.0 78.6 jit_solution(15975097089259965153)
XLA Ops:
  0.0 76.7 %shard_map.17 = bf16[512,512]{1,0:T(8,128)(2,1)} custom-call(bf16[512,512]{1,0:T(8,128)(2,1)} %tracks_ref.1), custom_call_target="tpu_custom_call" | custom-call | tf_op jit(solution)/shard_map/pallas_call | solution.py:414
  76.7 1.9 %copy.3 = bf16[512,512]{1,0:T(8,128)(2,1)} copy(bf16[512,512]{1,0:T(8,128)(2,1)} %shard_map.17) | data formatting | bytes 1048576

commit v3 on v2

--- a/solution.py
+++ b/solution.py
@@ -43,7 +43,8 @@
 
 
 def product(left, right):
-    return dot(left[0], right[0]) + (dot(left[0], right[1]) + dot(left[1], right[0]))
+    wide = jnp.concatenate([left[0], left[0], left[1]], axis=1)
+    return dot(wide, jnp.concatenate([right[0], right[1], right[0]], axis=0))
 
 
 def kernel(
@@ -241,6 +242,10 @@
         pass_back(1, part, last)
         lift(2, part)
         take_ring(3, part)
+        if part == 0:
+            send_ring(3, part)
+            pass_end(1, part)
+            pass_back(1, part, both(step_z > 0, inner))
         drop(3, part)
     pltpu.make_async_copy(line_in, line_in, line_recv).wait()
     total = line_out[...] + jnp.sum(line_in[...], axis=0)
@@ -256,11 +261,16 @@
 
     for dy, dx in PLANE:
         gather_hop(dy, dx).start()
-    for part in range(CHUNKS):
+    for part in range(1, CHUNKS):
         send_ring(3, part)
         pass_end(1, part)
         pass_back(1, part, both(step_z > 0, inner))
+    pass_ring(2, 0)
+    drop(2, 0)
     each(lambda part: pass_end(2, part))
+    pass_back(1, 0, step_z == 0)
+    pass_back(2, 0, step_z > 1)
+    lift(3, 0)
     others = full.at[core, pl.ds(0, PART * 15)]
     pltpu.make_async_copy(others, others, gather_recv).wait()
     whole = pltpu.make_async_remote_copy(
@@ -268,7 +278,7 @@
         device_id=mate, device_id_type=MESH,
     )
     whole.start()
-    for part in range(CHUNKS):
+    for part in range(1, CHUNKS):
         pass_ring(2, part)
         pass_back(1, part, step_z == 0)
         pass_back(2, part, step_z > 1)
@@ -308,15 +318,19 @@
         else:
             inverse[...] = product(split(inverse[...]), factor)
         iterate[...] = product(split(iterate[...]), split(product(factor, factor)))
-        if sweep == 1:
+        if sweep == 0:
             pass_ring(1, 0)
             drop(1, 0)
+            pass_end(3, 0)
+        if sweep == 1:
+            pass_ring(1, 1)
+            drop(1, 1)
+            pass_back(2, 0, step_z < 2)
         if sweep == 2:
-            pass_end(3, 0)
+            pass_end(3, 1)
+            pass_back(2, 1, step_z < 2)
     unscaled = product(split(inverse[...]), split(factor_of(iterate[...])))
     whitener[...] = unscaled / jnp.sqrt(frobenius)
-    pass_ring(1, 1)
-    drop(1, 1)
     weights = split(whitener[...])
     centre = jnp.concatenate([average[i : i + 1] for i in range(4)], axis=1)
     centred = keys[OWN].astype(F32) - centre
@@ -329,13 +343,14 @@
     ]
 
     def key_slot(n):
-        return sum(jnp.where(n == i, slot, 0) for i, slot in enumerate(order))
-
-    def score(n, high):
+        return order[n]
+
+    def score(n, high, own=False):
         found = lax.dot_general(
             queries[...], keys[key_slot(n)], (((1,), (1,)), ((), ())), preferred_element_type=F32
         )
-        found = jnp.where(both(diagonal, n == 0), -jnp.inf, found)
+        if own:
+            found = jnp.where(diagonal, -jnp.inf, found)
         scores[n] = found
         for i in range(4):
             high = jnp.maximum(high, found[:, 128 * i : 128 * (i + 1)])
@@ -344,7 +359,10 @@
     def attend(state, start, stop):
         before, totals = state
         high = jnp.broadcast_to(before, (ROWS, 128))
-        high = lax.fori_loop(start, stop, score, high)
+        if start == 0:
+            high = score(0, high, True)
+        for n in range(max(start, 1), stop):
+            high = score(n, high)
         highest = jnp.max(high, axis=1, keepdims=True)
         if start > 0:
             decay = jnp.exp2(before - highest)
@@ -359,11 +377,11 @@
                 totals = totals + wide[:, 128 * i : 128 * (i + 1)]
             return totals
 
-        return highest, lax.fori_loop(start, stop, spread, totals)
-
-    pass_end(3, 1)
+        for n in range(start, stop):
+            totals = spread(n, totals)
+        return highest, totals
+
     for part in range(CHUNKS):
-        pass_back(2, part, step_z < 2)
         take_side(3, part)
         take_side(2, part)
     start_mate_back(1)

time: 78.7 us -> 72 us (0.915)
  Pallas kernels: 76.7 us -> 70 us
    pallas_call x1, Pallas kernels: 76.7 us -> 70 us  [local(): pl.pallas_call(kernel, out_shape=jax.ShapeDtypeStruct((ROWS, WIDTH), BF16...]
where the time goes in v3:
time: 72 us; the launch traced here: 71.9 us
  Pallas kernels  70 us (97%)
  local copies, waits for them, and re-layouts  1.87 us (3%)
    pallas_call x1, Pallas kernels, local(): pl.pallas_call(kernel, out_shape=jax.ShapeDtypeStruct((ROWS, WIDTH), BF16...  70 us
    unnamed x1, local copies, waits for them, and re-layouts  1.87 us

profile of v3, /device:TPU:65, one launch (start us, length us, event | category | flops | bytes accessed | tf_op | source)
XLA Modules:
  0.0 71.9 jit_solution(9765880716058182455)
XLA Ops:
  0.0 70.0 %shard_map.17 = bf16[512,512]{1,0:T(8,128)(2,1)} custom-call(bf16[512,512]{1,0:T(8,128)(2,1)} %tracks_ref.1), custom_call_target="tpu_custom_call" | custom-call | tf_op jit(solution)/shard_map/pallas_call | solution.py:432
  70.0 1.9 %copy.3 = bf16[512,512]{1,0:T(8,128)(2,1)} copy(bf16[512,512]{1,0:T(8,128)(2,1)} %shard_map.17) | data formatting | bytes 1048576

commit v4 on v3

--- a/solution.py
+++ b/solution.py
@@ -271,6 +271,12 @@
     pass_back(1, 0, step_z == 0)
     pass_back(2, 0, step_z > 1)
     lift(3, 0)
+    for part in range(1, CHUNKS):
+        pass_ring(2, part)
+        pass_back(1, part, step_z == 0)
+        pass_back(2, part, step_z > 1)
+        lift(3, part)
+        drop(2, part)
     others = full.at[core, pl.ds(0, PART * 15)]
     pltpu.make_async_copy(others, others, gather_recv).wait()
     whole = pltpu.make_async_remote_copy(
@@ -278,12 +284,8 @@
         device_id=mate, device_id_type=MESH,
     )
     whole.start()
-    for part in range(1, CHUNKS):
-        pass_ring(2, part)
-        pass_back(1, part, step_z == 0)
-        pass_back(2, part, step_z > 1)
-        lift(3, part)
-        drop(2, part)
+    pass_ring(1, 0)
+    drop(1, 0)
     start_mate_back(0)
     whole.wait()
 
@@ -319,16 +321,19 @@
             inverse[...] = product(split(inverse[...]), factor)
         iterate[...] = product(split(iterate[...]), split(product(factor, factor)))
         if sweep == 0:
-            pass_ring(1, 0)
-            drop(1, 0)
             pass_end(3, 0)
-        if sweep == 1:
             pass_ring(1, 1)
             drop(1, 1)
+        if sweep == 1:
             pass_back(2, 0, step_z < 2)
+            pass_end(3, 1)
         if sweep == 2:
-            pass_end(3, 1)
             pass_back(2, 1, step_z < 2)
+            for part in range(CHUNKS):
+                take_side(3, part)
+                take_side(2, part)
+            start_mate_back(1)
+            start_mate_ring(2)
     unscaled = product(split(inverse[...]), split(factor_of(iterate[...])))
     whitener[...] = unscaled / jnp.sqrt(frobenius)
     weights = split(whitener[...])
@@ -381,21 +386,16 @@
             totals = spread(n, totals)
         return highest, totals
 
-    for part in range(CHUNKS):
-        take_side(3, part)
-        take_side(2, part)
-    start_mate_back(1)
-    start_mate_ring(2)
     each(lambda part: mate_back(0, part).wait_recv())
     weighted[...] = jnp.zeros_like(weighted)
     state = (jnp.full((ROWS, 1), -jnp.inf, F32), jnp.zeros((ROWS, 128), F32))
     state = attend(state, 0, 3)
     each(lambda part: mate_back(1, part).wait_recv())
     each(lambda part: mate_ring(2, part).wait_recv())
-    state = attend(state, 3, 7)
     each(lambda part: take_side(1, part))
     start_mate_ring(1)
     when(second, lambda: start_mate_ring(0))
+    state = attend(state, 3, 7)
     each(lambda part: take_ring(0, part))
     when(core == 0, lambda: start_mate_ring(0))
     each(lambda part: pass_back(3, part, step_z >= 0))

time: 72 us -> 70.9 us (0.985)
  Pallas kernels: 70 us -> 68.6 us
    pallas_call x1, Pallas kernels: 70 us -> 68.6 us  [local(): pl.pallas_call(kernel, out_shape=jax.ShapeDtypeStruct((ROWS, WIDTH), BF16...]
where the time goes in v4:
time: 70.9 us; the launch traced here: 70.5 us
  Pallas kernels  68.6 us (97%)
  local copies, waits for them, and re-layouts  1.87 us (3%)
    pallas_call x1, Pallas kernels, local(): pl.pallas_call(kernel, out_shape=jax.ShapeDtypeStruct((ROWS, WIDTH), BF16...  68.6 us
    unnamed x1, local copies, waits for them, and re-layouts  1.87 us

profile of v4, /device:TPU:65, one launch (start us, length us, event | category | flops | bytes accessed | tf_op | source)
XLA Modules:
  0.0 70.5 jit_solution(9630228668544317733)
XLA Ops:
  0.0 68.6 %shard_map.17 = bf16[512,512]{1,0:T(8,128)(2,1)} custom-call(bf16[512,512]{1,0:T(8,128)(2,1)} %tracks_ref.1), custom_call_target="tpu_custom_call" | custom-call | tf_op jit(solution)/shard_map/pallas_call | solution.py:432
  68.6 1.9 %copy.3 = bf16[512,512]{1,0:T(8,128)(2,1)} copy(bf16[512,512]{1,0:T(8,128)(2,1)} %shard_map.17) | data formatting | bytes 1048576
